TPU v7x, 512 devices: a whole 4x4x16 slice. The times are simulated.
512 devices in a mesh: orb: 8 (over y, x_lo), grid: 64 (over x_hi, z, core).
Axes of the slice: x: 4 (x_hi: 2, x_lo: 2; x = x_hi * 2 + x_lo), y: 4, z: 16, core: 2. Of those that a mesh axis runs over, the one named last changes fastest.
Arguments:
- random_orbitals: float32 [8, 256, 256, 256], P('orb', 'grid'), may hold values from -6 to 6
- potential: float32 [256, 256, 256], P('grid'), may hold values from -1.5 to 0.5
- sphere_cells: int32 [1024, 2, 128], P('grid'), may hold values from 0 to 65535, as said below
- projectors: float32 [1024, 4, 128], P('grid'), may hold values from -0.9 to 0.9
- kb_energy: float32 [4], replicated, may hold values from 0.5 to 1.5
- cheb_coef: float32 [3], replicated, may hold values from 0.5 to 1.5
Outputs:
- density: float32 [256, 256, 256], P('grid')
Inputs may be any that keep to these rules, and one draw needn't show every extreme that they name: `sphere_cells`: for each atom a the 128 points are distinct cells: the 128 offsets (dz, dy, dx) with |dz|, |dy|, |dx| <= 3 nearest to the atom's centre, ties broken by the order of (dz, dy, dx) from smallest to largest, added to the centre with periodic wrap along each dimension; row 0 holds the z-plane and row 1 the cell y * 256 + x. The centre's z lies in the slab of planes (a // 16) * 4 to (a // 16) * 4 + 3. Spheres of different atoms may share cells.
All inputs are finite; a program needn't handle non-finite values.
Results may differ from a plain program's by a relative error of at most 0.0002.
Values sent between devices are 32-bit elements; how exact they have to be, the bound alone decides.
A program may use at most 64 MiB of HBM per device.

v0:
```python
import math
import jax
import jax.numpy as jnp
from jax import lax
from jax.sharding import PartitionSpec as P

REACH = 3
PRECISE = lax.Precision.HIGHEST
CENTRE = 2.0
HALF_RANGE = 4.0


def with_halo(cells, sides, width):
    for axis, dim in sides:
        count = lax.axis_size(axis)
        head = lax.slice_in_dim(cells, 0, width, axis=dim)
        tail = lax.slice_in_dim(cells, cells.shape[dim] - width, cells.shape[dim], axis=dim)
        cells = jnp.concatenate(
            [
                lax.ppermute(tail, axis, [(i, (i + 1) % count) for i in range(count)]),
                cells,
                lax.ppermute(head, axis, [((i + 1) % count, i) for i in range(count)]),
            ],
            axis=dim,
        )
    return cells


def from_behind(block, axis, distance):
    devices = range(lax.axis_size(axis))
    route = [((i - distance) % len(devices), i) for i in devices]
    return lax.ppermute(block, axis, route)


def kinetic_table(length):
    places = jnp.arange(length)
    offset = places[:, None] - places[None, :]
    parity = jnp.where(offset % 2 == 0, 1.0, -1.0).astype(jnp.float32)
    angle_half = offset.astype(jnp.float32) * (math.pi / length)
    sine = jnp.where(offset == 0, 1.0, jnp.sin(angle_half))
    off_diag = parity / (2.0 * sine * sine)
    on_diag = jnp.float32(length * length / 12.0 + 1.0 / 6.0)
    return jnp.where(offset == 0, on_diag, off_diag) * (4.0 / (length * length))


def local(random_orbitals, potential, sphere_cells, projectors, kb_energy, cheb_coef):
    grid_count = lax.axis_size("grid")
    grid_pos = lax.axis_index("grid")
    planes = potential.shape[0]
    rows_y = potential.shape[1]
    cols_x = potential.shape[2]
    all_planes = planes * grid_count
    plane_cells = rows_y * cols_x
    first_plane = grid_pos * planes
    orb_count = random_orbitals.shape[0]
    per_dev = sphere_cells.shape[0]
    kinetic_x = kinetic_table(cols_x)
    kinetic_y = kinetic_table(rows_y)
    kinetic_z = kinetic_table(all_planes)

    def along_z(columns):
        turned = jnp.einsum("ozyx,zw->owyx", columns, kinetic_z, precision=PRECISE)
        return lax.all_to_all(turned, "grid", split_axis=1, concat_axis=2, tiled=True)

    z_glob = sphere_cells[:, 0, :]
    in_plane = sphere_cells[:, 1, :]
    local_plane = (z_glob - first_plane + REACH) % all_planes
    ghost_index = (local_plane * plane_cells + in_plane).reshape(-1)

    def nonlocal_term(vector):
        extended = with_halo(vector, (("grid", 1),), REACH)
        flattened = extended.reshape(orb_count, -1)
        values = flattened[:, ghost_index].reshape(orb_count, per_dev, -1)
        coeffs = jnp.einsum("oaj,apj->oap", values, projectors, precision=PRECISE) * kb_energy
        spread = jnp.einsum("oap,apj->oaj", coeffs, projectors, precision=PRECISE).reshape(
            orb_count, -1
        )
        placed = jnp.zeros_like(flattened).at[:, ghost_index].add(spread).reshape(extended.shape)
        lower_rim = placed[:, :REACH]
        upper_rim = placed[:, REACH + planes :]
        from_above = from_behind(lower_rim, "grid", -1)
        from_below = from_behind(upper_rim, "grid", 1)
        interior = placed[:, REACH : REACH + planes]
        interior = interior.at[:, :REACH].add(from_below)
        interior = interior.at[:, planes - REACH :].add(from_above)
        return interior

    def apply_hamiltonian(vector):
        kinetic = jnp.dot(vector.reshape(-1, cols_x), kinetic_x, precision=PRECISE).reshape(
            vector.shape
        )
        kinetic = kinetic + jnp.einsum("ozyx,yw->ozwx", vector, kinetic_y, precision=PRECISE)
        kinetic = kinetic + along_z(
            lax.all_to_all(vector, "grid", split_axis=2, concat_axis=1, tiled=True)
        )
        summed = kinetic + potential * vector + nonlocal_term(vector)
        return (summed - CENTRE * vector) / HALF_RANGE

    first_term = apply_hamiltonian(random_orbitals)
    second_term = 2.0 * apply_hamiltonian(first_term) - random_orbitals
    filtered = (
        cheb_coef[0] * random_orbitals + cheb_coef[1] * first_term + cheb_coef[2] * second_term
    )
    group_density = jnp.sum(filtered * filtered, axis=0)
    density = lax.psum(group_density, "orb")
    return density / (orb_count * lax.axis_size("orb"))


def solution(mesh):
    in_specs = (
        P("orb", "grid", None, None),
        P("grid", None, None),
        P("grid", None, None),
        P("grid", None, None),
        P(),
        P(),
    )
    out_specs = P("grid", None, None)
    return jax.shard_map(local, mesh=mesh, in_specs=in_specs, out_specs=out_specs, check_vma=False)
```

profile of v0, /device:TPU:4, one launch (start us, length us, event | category | flops | bytes accessed | tf_op | source)
XLA Modules:
  0.0 507.4 jit_solution(14557212406994386126)
XLA Ops:
  8.4 70.6 %all_to_all.66 = f32[1,4,256,256]{3,1,0,2:T(4,128)S(1)} all-to-all(f32[1,4,256,256]{3,1,0,2:T(4,128)S(1)} %copy.20), channel_id=1, replica_groups=mesh['orb'=8,'grid'=64] {'grid'}, dimensions={2} | all-to-all | bytes 2097152 | tf_op jit(solution)/shard_map/all_to_all | solution.py:94
  83.3 9.8 %all-to-all-start.1 = ((f32[1,256,4,256]{3,2,0,1:T(4,128)}), f32[1,256,4,256]{3,2,0,1:T(4,128)}, u32[]{:S(2)}, u32[]{:S(2)}) async-start(f32[1,256,4,256]{3,2,0,1:T(4,128)} %copy.22), calls=%async_computation.1 | async-start | bytes 2097152 | tf_op jit(solution)/shard_map/all_to_all | solution.py:63
  96.2 7.1 %collective-permute-start.1 = (f32[1,3,256,256]{3,2,1,0:T(8,128)S(1)}, f32[1,3,256,256]{3,2,1,0:T(8,128)S(1)}, u32[]{:S(2)}, u32[]{:S(2)}) collective-permute-start(f32[1,3,256,256]{3,2,1,0:T(8,128)S(1)} %get-tuple-element.60), channel_id=1, source_target_pairs={{1,0},{2,1},{3,2},{4,3},{5,4},{6,5},{7,6},{8,7},{9,8},{10,9},{11,1... | collective-permute-start | bytes 2359304 | tf_op jit(solution)/shard_map/ppermute | solution.py:22
  103.4 46.4 %collective-permute-done = f32[1,3,256,256]{3,2,1,0:T(8,128)S(1)} collective-permute-done((f32[1,3,256,256]{3,2,1,0:T(8,128)}, f32[1,3,256,256]{3,2,1,0:T(8,128)S(1)}, u32[]{:S(2)}, u32[]{:S(2)}) %collective-permute-start) | collective-permute-done | bytes 786464 | tf_op jit(solution)/shard_map/ppermute | solution.py:20
  151.3 11.8 %gather_fusion = f32[2048]{0:T(1024)S(1)} fusion(f32[655360]{0:T(1024)S(1)} %bitcast.161, s32[2048]{0:T(1024)S(1)} %broadcast_clamp_fusion), kind=kCustom, calls=%fused_computation | custom fusion | bytes 24576 | tf_op jit(solution)/shard_map/gather | solution.py:73
  163.7 11.9 %scatter_custom_fusion = f32[655360]{0:T(1024)S(1)} fusion(s32[2048]{0:T(1024)S(1)} %bitcast.173, f32[2048]{0:T(1024)S(1)} %bitcast.182, f32[]{:T(128)} %constant.158.clone.1), kind=kCustom, calls=%fused_computation.14 | custom fusion | flops 2048 | bytes 2621444 | tf_op jit(solution)/shard_map/scatter-add | solution.py:78
  177.5 2.8 fusion.109
  182.2 7.4 %collective-permute-start.3 = (f32[1,3,256,256]{3,2,1,0:T(8,128)}, f32[1,3,256,256]{3,2,1,0:T(8,128)}, u32[]{:S(2)}, u32[]{:S(2)}) collective-permute-start(f32[1,3,256,256]{3,2,1,0:T(8,128)} %get-tuple-element.55), channel_id=1, source_target_pairs={{1,0},{2,1},{3,2},{4,3},{5,4},{6,5},{7,6},{8,7},{9,8},{10,9},{11,1... | collective-permute-start | bytes 2359304 | tf_op jit(solution)/shard_map/ppermute | solution.py:32
  193.1 4.4 collective-permute-done.2
  203.4 5.2 %broadcast_multiply_fusion.1 = (f32[1,4,256,256]{3,2,1,0:T(8,128)S(1)}, f32[1,4,256,256]{3,2,1,0:T(8,128)}) fusion(f32[1,4,256,256]{3,2,1,0:T(8,128)S(1)} %copy-done.2, f32[1,4,256,256]{3,2,1,0:T(8,128)S(1)} %fusion.25, f32[4,256,256]{2,1,0:T(8,128)} %param.15, f32[1,4,256,256]{3,2,1,0:T(8,128)} %all_to_all.54, f32[1,4,256,256]{3,2,1,0:T(8,128)} %bitcast.165), kind=kOutput, calls=%fused_computation.50 | convolution fusion | flops 808910848 | bytes 7340032 | tf_op jit(solution)/shard_map/ozyx,yw->ozwx/dot_general | solution.py:92
  209.2 63.0 %all_to_all.67 = f32[1,4,256,256]{3,1,0,2:T(4,128)S(1)} all-to-all(f32[1,4,256,256]{3,1,0,2:T(4,128)S(1)} %copy.25), channel_id=1, replica_groups=mesh['orb'=8,'grid'=64] {'grid'}, dimensions={2} | all-to-all | bytes 2097152 | tf_op jit(solution)/shard_map/all_to_all | solution.py:94
  276.6 9.6 %all-to-all-start.3 = ((f32[1,256,4,256]{3,2,0,1:T(4,128)}), f32[1,256,4,256]{3,2,0,1:T(4,128)}, u32[]{:S(2)}, u32[]{:S(2)}) async-start(f32[1,256,4,256]{3,2,0,1:T(4,128)} %copy.27), calls=%async_computation.3 | async-start | bytes 2097152 | tf_op jit(solution)/shard_map/all_to_all | solution.py:63
  288.4 7.3 %collective-permute-start.5 = (f32[1,3,256,256]{3,2,1,0:T(8,128)S(1)}, f32[1,3,256,256]{3,2,1,0:T(8,128)S(1)}, u32[]{:S(2)}, u32[]{:S(2)}) collective-permute-start(f32[1,3,256,256]{3,2,1,0:T(8,128)S(1)} %get-tuple-element.58), channel_id=1, source_target_pairs={{1,0},{2,1},{3,2},{4,3},{5,4},{6,5},{7,6},{8,7},{9,8},{10,9},{11,1... | collective-permute-start | bytes 2359304 | tf_op jit(solution)/shard_map/ppermute | solution.py:22
  295.8 47.1 %collective-permute-done.4 = f32[1,3,256,256]{3,2,1,0:T(8,128)S(1)} collective-permute-done((f32[1,3,256,256]{3,2,1,0:T(8,128)S(1)}, f32[1,3,256,256]{3,2,1,0:T(8,128)S(1)}, u32[]{:S(2)}, u32[]{:S(2)}) %collective-permute-start.4) | collective-permute-done | bytes 786464 | tf_op jit(solution)/shard_map/ppermute | solution.py:20
  344.5 11.8 %gather_fusion.1 = f32[2048]{0:T(1024)S(1)} fusion(f32[655360]{0:T(1024)S(1)} %bitcast.160, s32[2048]{0:T(1024)S(1)} %broadcast_clamp_fusion), kind=kCustom, calls=%fused_computation.1 | custom fusion | bytes 24576 | tf_op jit(solution)/shard_map/gather | solution.py:73
  356.8 12.9 %scatter_custom_fusion.1 = f32[655360]{0:T(1024)} fusion(s32[2048]{0:T(1024)S(1)} %bitcast.174, f32[2048]{0:T(1024)S(1)} %bitcast.181, f32[]{:T(128)} %constant.158.clone.1), kind=kCustom, calls=%fused_computation.12 | custom fusion | flops 2048 | bytes 2621444 | tf_op jit(solution)/shard_map/scatter-add | solution.py:78
  369.7 2.7 reshape.296
  374.7 7.3 %collective-permute-start.7 = (f32[1,3,256,256]{3,2,1,0:T(8,128)S(1)}, f32[1,3,256,256]{3,2,1,0:T(8,128)S(1)}, u32[]{:S(2)}, u32[]{:S(2)}) collective-permute-start(f32[1,3,256,256]{3,2,1,0:T(8,128)S(1)} %get-tuple-element.53), channel_id=1, source_target_pairs={{1,0},{2,1},{3,2},{4,3},{5,4},{6,5},{7,6},{8,7},{9,8},{10,9},{11,1... | collective-permute-start | bytes 2359304 | tf_op jit(solution)/shard_map/ppermute | solution.py:32
  383.3 3.1 convolution_bitcast_fusion.1
  387.4 2.3 collective-permute-done.6
  393.7 2.5 copy.46
  396.2 2.6 all_to_all.61
  398.8 6.6 %fusion.21 = f32[4,256,256]{2,1,0:T(8,128)} fusion(f32[1,4,256,256]{3,2,1,0:T(8,128)S(1)} %copy-done.3, f32[1,4,256,256]{3,2,1,0:T(8,128)} %fusion.23, f32[4,256,256]{2,1,0:T(8,128)S(1)} %copy-done.4, f32[1,4,256,256]{3,2,1,0:T(8,128)S(1)} %copy-done.6, f32[]{:T(128)} %bitcast.28, f32[]{:T(128)} %bitcast.27, f32[]{:T(128)} %bitcast, ...), kind=kOutput, calls=%fused_computation.35 | convolution fusion | flops 811270144 | bytes 7340044 | tf_op jit(solution)/shard_map/dot_general | solution.py:89
  405.3 92.9 %all-reduce.2.cloned.1.call-done = f32[4,256,256]{2,1,0:T(8,128)} async-done(((f32[4,256,256]{2,1,0:T(8,128)}), f32[4,256,256]{2,1,0:T(8,128)}) %all-reduce.2.cloned.1.call-update) | async-done | bytes 1048592 | tf_op jit(solution)/shard_map/psum | solution.py:105
  (71 shorter events, 43.8 us)
Async XLA Ops:
  6.5 156.6 %copy-start = (f32[16,4,128]{2,1,0:T(4,128)S(1)}, f32[16,4,128]{2,1,0:T(4,128)}, u32[]{:S(2)}) copy-start(f32[16,4,128]{2,1,0:T(4,128)} %param.17) | copy-start | bytes 98308
  81.6 11.4 %copy-start.1 = (f32[1,4,256,256]{3,2,1,0:T(8,128)S(1)}, f32[1,4,256,256]{3,2,1,0:T(8,128)}, u32[]{:S(2)}) copy-start(f32[1,4,256,256]{3,2,1,0:T(8,128)} %param.14) | copy-start | bytes 3145732
  83.3 20.0 %copy-start.7 = (s32[16,2,128]{2,1,0:T(2,128)S(1)}, s32[16,2,128]{2,1,0:T(2,128)}, u32[]{:S(2)}) copy-start(s32[16,2,128]{2,1,0:T(2,128)} %param.16) | copy-start | bytes 49156
  83.3 117.3 %all-to-all-start.1 = ((f32[1,256,4,256]{3,2,0,1:T(4,128)}), f32[1,256,4,256]{3,2,0,1:T(4,128)}, u32[]{:S(2)}, u32[]{:S(2)}) async-start(f32[1,256,4,256]{3,2,0,1:T(4,128)} %copy.22), calls=%async_computation.1 | async-start | bytes 2097152 | tf_op jit(solution)/shard_map/all_to_all | solution.py:63
  94.1 55.6 %collective-permute-start = (f32[1,3,256,256]{3,2,1,0:T(8,128)}, f32[1,3,256,256]{3,2,1,0:T(8,128)S(1)}, u32[]{:S(2)}, u32[]{:S(2)}) collective-permute-start(f32[1,3,256,256]{3,2,1,0:T(8,128)} %get-tuple-element.59), channel_id=1, source_target_pairs={{0,1},{1,2},{2,3},{3,4},{4,5},{5,6},{6,7},{7,8},{8,9},{9,10},{10,1... | collective-permute-start | bytes 2359304 | tf_op jit(solution)/shard_map/ppermute | solution.py:20
  96.2 53.6 %collective-permute-start.1 = (f32[1,3,256,256]{3,2,1,0:T(8,128)S(1)}, f32[1,3,256,256]{3,2,1,0:T(8,128)S(1)}, u32[]{:S(2)}, u32[]{:S(2)}) collective-permute-start(f32[1,3,256,256]{3,2,1,0:T(8,128)S(1)} %get-tuple-element.60), channel_id=1, source_target_pairs={{1,0},{2,1},{3,2},{4,3},{5,4},{6,5},{7,6},{8,7},{9,8},{10,9},{11,1... | collective-permute-start | bytes 2359304 | tf_op jit(solution)/shard_map/ppermute | solution.py:22
  151.3 12.1 %copy-start.9 = (f32[4]{0:T(128)S(1)}, f32[4]{0:T(128)}, u32[]{:S(2)}) copy-start(f32[4]{0:T(128)} %param.18) | copy-start | bytes 52
  177.5 12.2 %copy-start.2 = (f32[1,4,256,256]{3,2,1,0:T(8,128)S(1)}, f32[1,4,256,256]{3,2,1,0:T(8,128)}, u32[]{:S(2)}) copy-start(f32[1,4,256,256]{3,2,1,0:T(8,128)} %param.14) | copy-start | bytes 3145732
  180.3 17.2 %collective-permute-start.2 = (f32[1,3,256,256]{3,2,1,0:T(8,128)}, f32[1,3,256,256]{3,2,1,0:T(8,128)}, u32[]{:S(2)}, u32[]{:S(2)}) collective-permute-start(f32[1,3,256,256]{3,2,1,0:T(8,128)} %get-tuple-element.56), channel_id=1, source_target_pairs={{63,0},{0,1},{1,2},{2,3},{3,4},{4,5},{5,6},{6,7},{7,8},{8,9},{9,10... | collective-permute-start | bytes 2359304 | tf_op jit(solution)/shard_map/ppermute | solution.py:32
  182.2 17.1 %collective-permute-start.3 = (f32[1,3,256,256]{3,2,1,0:T(8,128)}, f32[1,3,256,256]{3,2,1,0:T(8,128)}, u32[]{:S(2)}, u32[]{:S(2)}) collective-permute-start(f32[1,3,256,256]{3,2,1,0:T(8,128)} %get-tuple-element.55), channel_id=1, source_target_pairs={{1,0},{2,1},{3,2},{4,3},{5,4},{6,5},{7,6},{8,7},{9,8},{10,9},{11,1... | collective-permute-start | bytes 2359304 | tf_op jit(solution)/shard_map/ppermute | solution.py:32
  191.8 5.8 %slice-start = ((f32[1,10,256,256]{3,2,1,0:T(8,128)}), f32[1,4,256,256]{3,2,1,0:T(8,128)S(1)}, s32[]{:S(2)}) async-start(f32[1,10,256,256]{3,2,1,0:T(8,128)} %reshape.291), calls=%async_computation.5 | async-start | bytes 2097152 | tf_op jit(solution)/shard_map/slice | solution.py:83
  276.6 117.1 %all-to-all-start.3 = ((f32[1,256,4,256]{3,2,0,1:T(4,128)}), f32[1,256,4,256]{3,2,0,1:T(4,128)}, u32[]{:S(2)}, u32[]{:S(2)}) async-start(f32[1,256,4,256]{3,2,0,1:T(4,128)} %copy.27), calls=%async_computation.3 | async-start | bytes 2097152 | tf_op jit(solution)/shard_map/all_to_all | solution.py:63
  286.2 212.0 %all-reduce.2.cloned.1.call-start = ((), (), s32[]{:S(2)}) async-start(), calls=%async_computation.4 | async-start | bytes 2097152 | tf_op jit(solution)/shard_map/psum | solution.py:105
  286.4 56.5 %collective-permute-start.4 = (f32[1,3,256,256]{3,2,1,0:T(8,128)S(1)}, f32[1,3,256,256]{3,2,1,0:T(8,128)S(1)}, u32[]{:S(2)}, u32[]{:S(2)}) collective-permute-start(f32[1,3,256,256]{3,2,1,0:T(8,128)S(1)} %get-tuple-element.57), channel_id=1, source_target_pairs={{0,1},{1,2},{2,3},{3,4},{4,5},{5,6},{6,7},{7,8},{8,9},{9,10},{10,1... | collective-permute-start | bytes 2359304 | tf_op jit(solution)/shard_map/ppermute | solution.py:20
  288.4 54.4 %collective-permute-start.5 = (f32[1,3,256,256]{3,2,1,0:T(8,128)S(1)}, f32[1,3,256,256]{3,2,1,0:T(8,128)S(1)}, u32[]{:S(2)}, u32[]{:S(2)}) collective-permute-start(f32[1,3,256,256]{3,2,1,0:T(8,128)S(1)} %get-tuple-element.58), channel_id=1, source_target_pairs={{1,0},{2,1},{3,2},{4,3},{5,4},{6,5},{7,6},{8,7},{9,8},{10,9},{11,1... | collective-permute-start | bytes 2359304 | tf_op jit(solution)/shard_map/ppermute | solution.py:22
  372.5 9.5 %copy-start.8 = (f32[3]{0:T(128)S(1)}, f32[3]{0:T(128)}, u32[]{:S(2)}) copy-start(f32[3]{0:T(128)} %param.19) | copy-start | bytes 40
  372.5 10.8 %copy-start.5 = (f32[1,4,256,256]{3,2,1,0:T(8,128)S(1)}, f32[1,4,256,256]{3,2,1,0:T(8,128)}, u32[]{:S(2)}) copy-start(f32[1,4,256,256]{3,2,1,0:T(8,128)} %get-tuple-element.65) | copy-start | bytes 3145732
  372.7 17.1 %collective-permute-start.6 = (f32[1,3,256,256]{3,2,1,0:T(8,128)S(1)}, f32[1,3,256,256]{3,2,1,0:T(8,128)S(1)}, u32[]{:S(2)}, u32[]{:S(2)}) collective-permute-start(f32[1,3,256,256]{3,2,1,0:T(8,128)S(1)} %get-tuple-element.54), channel_id=1, source_target_pairs={{63,0},{0,1},{1,2},{2,3},{3,4},{4,5},{5,6},{6,7},{7,8},{8,9},{9,10... | collective-permute-start | bytes 2359304 | tf_op jit(solution)/shard_map/ppermute | solution.py:32
  374.7 16.8 %collective-permute-start.7 = (f32[1,3,256,256]{3,2,1,0:T(8,128)S(1)}, f32[1,3,256,256]{3,2,1,0:T(8,128)S(1)}, u32[]{:S(2)}, u32[]{:S(2)}) collective-permute-start(f32[1,3,256,256]{3,2,1,0:T(8,128)S(1)} %get-tuple-element.53), channel_id=1, source_target_pairs={{1,0},{2,1},{3,2},{4,3},{5,4},{6,5},{7,6},{8,7},{9,8},{10,9},{11,1... | collective-permute-start | bytes 2359304 | tf_op jit(solution)/shard_map/ppermute | solution.py:32
  393.6 5.1 %copy-start.3 = (f32[1,4,256,256]{3,2,1,0:T(8,128)S(1)}, f32[1,4,256,256]{3,2,1,0:T(8,128)}, u32[]{:S(2)}) copy-start(f32[1,4,256,256]{3,2,1,0:T(8,128)} %param.14) | copy-start | bytes 3145732
  393.6 5.1 %copy-start.4 = (f32[4,256,256]{2,1,0:T(8,128)S(1)}, f32[4,256,256]{2,1,0:T(8,128)}, u32[]{:S(2)}) copy-start(f32[4,256,256]{2,1,0:T(8,128)} %param.15) | copy-start | bytes 3145732
  393.7 5.1 %copy-start.6 = (f32[1,4,256,256]{3,2,1,0:T(8,128)S(1)}, f32[1,4,256,256]{3,2,1,0:T(8,128)}, u32[]{:S(2)}) copy-start(f32[1,4,256,256]{3,2,1,0:T(8,128)} %get-tuple-element.65) | copy-start | bytes 3145732
Sparse Core Ops, SparseCore 0:
  405.5 92.7 all-reduce.1
where the time goes:
time: 508 us; the launch traced here: 507 us
  waiting for transfers between devices  194 us (38%)
  blocking collectives  134 us (26%)
  starting transfers between devices  56.7 us (11%)
  local copies, waits for them, and re-layouts  52.9 us (10%)
  other arithmetic  33.6 us (7%)
  matrix products  22.1 us (4%)
  between operations  14.4 us (3%)
    all_to_all x2, blocking collectives, apply_hamiltonian(): lax.all_to_all(vector, 'grid', split_axis=2, concat_axis=1, tiled=True)  134 us
    ppermute x2, waiting for transfers between devices, with_halo(): lax.ppermute(tail, axis, [(i, (i + 1) % count) for i in range(count)])  93.5 us
    psum x1, waiting for transfers between devices, local(): density = lax.psum(group_density, 'orb')  92.9 us
    scatter-add x2, other arithmetic, nonlocal_term(): jnp.zeros_like(flattened).at[:, ghost_index].add(spread)  24.9 us
    gather x2, local copies, waits for them, and re-layouts, nonlocal_term(): values = flattened[:, ghost_index].reshape(orb_count, per_dev, -1)  23.6 us
    all_to_all x2, starting transfers between devices, along_z(): lax.all_to_all(turned, 'grid', split_axis=1, concat_axis=2, tiled=True)  19.4 us
    ppermute x4, starting transfers between devices, from_behind(): return lax.ppermute(block, axis, route)  18.7 us
    ppermute x2, starting transfers between devices, with_halo(): lax.ppermute(head, axis, [((i + 1) % count, i) for i in range(count)])  14.5 us
  transfers between devices with their start and end apart: 11, of which 7 were waited for; matrix products, arithmetic and copies ran while one was open for 15% of the time, Pallas kernels for 0%

commit v1 on v0

--- a/solution.py
+++ b/solution.py
@@ -3,6 +3,7 @@
 import jax.numpy as jnp
 from jax import lax
 from jax.sharding import PartitionSpec as P
+from jax.lax import all_gather
 
 REACH = 3
 PRECISE = lax.Precision.HIGHEST
@@ -102,7 +103,8 @@
         cheb_coef[0] * random_orbitals + cheb_coef[1] * first_term + cheb_coef[2] * second_term
     )
     group_density = jnp.sum(filtered * filtered, axis=0)
-    density = lax.psum(group_density, "orb")
+    halves_pair = lambda frame_in: jnp.sum(all_gather(frame_in, axis_name="orb"), axis=0)
+    density = halves_pair(group_density)
     return density / (orb_count * lax.axis_size("orb"))
 
 

time: 508 us -> 592 us (1.17)
  the two profiles are of different devices: /device:TPU:4 before, /device:TPU:1 now
where the time goes in v1:
time: 592 us; the launch traced here: 591 us
  waiting for transfers between devices  280 us (47%)
  blocking collectives  138 us (23%)
  local copies, waits for them, and re-layouts  52.9 us (9%)
  starting transfers between devices  47.4 us (8%)
  other arithmetic  36.5 us (6%)
  matrix products  22.1 us (4%)
  between operations  14.4 us (2%)
    all_gather x1, waiting for transfers between devices, local(): all_gather(frame_in, axis_name='orb')  177 us
    all_to_all x2, blocking collectives, apply_hamiltonian(): lax.all_to_all(vector, 'grid', split_axis=2, concat_axis=1, tiled=True)  138 us
    ppermute x2, waiting for transfers between devices, with_halo(): lax.ppermute(tail, axis, [(i, (i + 1) % count) for i in range(count)])  94.7 us
    scatter-add x2, other arithmetic, nonlocal_term(): jnp.zeros_like(flattened).at[:, ghost_index].add(spread)  25 us
    gather x2, local copies, waits for them, and re-layouts, nonlocal_term(): values = flattened[:, ghost_index].reshape(orb_count, per_dev, -1)  23.6 us
    all_to_all x2, starting transfers between devices, along_z(): lax.all_to_all(turned, 'grid', split_axis=1, concat_axis=2, tiled=True)  19.8 us
    ppermute x4, starting transfers between devices, from_behind(): return lax.ppermute(block, axis, route)  16.5 us
  transfers between devices with their start and end apart: 11, of which 7 were waited for; matrix products, arithmetic and copies ran while one was open for 13% of the time, Pallas kernels for 0%

profile of v1, /device:TPU:1, one launch (start us, length us, event | category | flops | bytes accessed | tf_op | source)
XLA Modules:
  0.0 591.3 jit_solution(7609782320106821783)
XLA Ops:
  8.4 71.3 %all_to_all.66 = f32[1,4,256,256]{3,1,0,2:T(4,128)S(1)} all-to-all(f32[1,4,256,256]{3,1,0,2:T(4,128)S(1)} %copy.20), channel_id=1, replica_groups=mesh['orb'=8,'grid'=64] {'grid'}, dimensions={2} | all-to-all | bytes 2097152 | tf_op jit(solution)/shard_map/all_to_all | solution.py:95
  84.0 10.0 %all-to-all-start.1 = ((f32[1,256,4,256]{3,2,0,1:T(4,128)}), f32[1,256,4,256]{3,2,0,1:T(4,128)}, u32[]{:S(2)}, u32[]{:S(2)}) async-start(f32[1,256,4,256]{3,2,0,1:T(4,128)} %copy.22), calls=%async_computation.1 | async-start | bytes 2097152 | tf_op jit(solution)/shard_map/all_to_all | solution.py:64
  95.0 3.5 collective-permute-start
  100.6 47.1 %collective-permute-done = f32[1,3,256,256]{3,2,1,0:T(8,128)S(1)} collective-permute-done((f32[1,3,256,256]{3,2,1,0:T(8,128)}, f32[1,3,256,256]{3,2,1,0:T(8,128)S(1)}, u32[]{:S(2)}, u32[]{:S(2)}) %collective-permute-start) | collective-permute-done | bytes 786464 | tf_op jit(solution)/shard_map/ppermute | solution.py:21
  151.2 11.8 %gather_fusion = f32[2048]{0:T(1024)S(1)} fusion(f32[655360]{0:T(1024)S(1)} %bitcast.157, s32[2048]{0:T(1024)S(1)} %broadcast_clamp_fusion), kind=kCustom, calls=%fused_computation | custom fusion | bytes 24576 | tf_op jit(solution)/shard_map/gather | solution.py:74
  163.6 12.0 %scatter_custom_fusion = f32[655360]{0:T(1024)S(1)} fusion(s32[2048]{0:T(1024)S(1)} %bitcast.169, f32[2048]{0:T(1024)S(1)} %bitcast.178, f32[]{:T(128)} %constant.158.clone.1), kind=kCustom, calls=%fused_computation.14 | custom fusion | flops 2048 | bytes 2621444 | tf_op jit(solution)/shard_map/scatter-add | solution.py:79
  177.5 2.8 fusion.108
  182.6 6.0 %collective-permute-start.3 = (f32[1,3,256,256]{3,2,1,0:T(8,128)}, f32[1,3,256,256]{3,2,1,0:T(8,128)}, u32[]{:S(2)}, u32[]{:S(2)}) collective-permute-start(f32[1,3,256,256]{3,2,1,0:T(8,128)} %get-tuple-element.55), channel_id=1, source_target_pairs={{1,0},{2,1},{3,2},{4,3},{5,4},{6,5},{7,6},{8,7},{9,8},{10,9},{11,1... | collective-permute-start | bytes 2359304 | tf_op jit(solution)/shard_map/ppermute | solution.py:33
  193.5 3.0 collective-permute-done.3
  200.6 5.2 broadcast_multiply_fusion.1
  206.4 66.5 %all_to_all.67 = f32[1,4,256,256]{3,1,0,2:T(4,128)S(1)} all-to-all(f32[1,4,256,256]{3,1,0,2:T(4,128)S(1)} %copy.25), channel_id=1, replica_groups=mesh['orb'=8,'grid'=64] {'grid'}, dimensions={2} | all-to-all | bytes 2097152 | tf_op jit(solution)/shard_map/all_to_all | solution.py:95
  277.3 9.8 %all-to-all-start.3 = ((f32[1,256,4,256]{3,2,0,1:T(4,128)}), f32[1,256,4,256]{3,2,0,1:T(4,128)}, u32[]{:S(2)}, u32[]{:S(2)}) async-start(f32[1,256,4,256]{3,2,0,1:T(4,128)} %copy.27), calls=%async_computation.3 | async-start | bytes 2097152 | tf_op jit(solution)/shard_map/all_to_all | solution.py:64
  287.3 3.5 collective-permute-start.4
  293.0 47.6 %collective-permute-done.4 = f32[1,3,256,256]{3,2,1,0:T(8,128)S(1)} collective-permute-done((f32[1,3,256,256]{3,2,1,0:T(8,128)S(1)}, f32[1,3,256,256]{3,2,1,0:T(8,128)S(1)}, u32[]{:S(2)}, u32[]{:S(2)}) %collective-permute-start.4) | collective-permute-done | bytes 786464 | tf_op jit(solution)/shard_map/ppermute | solution.py:21
  344.4 11.8 %gather_fusion.1 = f32[2048]{0:T(1024)S(1)} fusion(f32[655360]{0:T(1024)S(1)} %bitcast.156, s32[2048]{0:T(1024)S(1)} %broadcast_clamp_fusion), kind=kCustom, calls=%fused_computation.1 | custom fusion | bytes 24576 | tf_op jit(solution)/shard_map/gather | solution.py:74
  356.7 13.0 %scatter_custom_fusion.1 = f32[655360]{0:T(1024)} fusion(s32[2048]{0:T(1024)S(1)} %bitcast.170, f32[2048]{0:T(1024)S(1)} %bitcast.177, f32[]{:T(128)} %constant.158.clone.1), kind=kCustom, calls=%fused_computation.12 | custom fusion | flops 2048 | bytes 2621444 | tf_op jit(solution)/shard_map/scatter-add | solution.py:79
  369.7 2.7 reshape.297
  375.1 5.8 collective-permute-start.7
  382.1 3.1 convolution_bitcast_fusion.1
  390.9 2.5 copy.46
  393.4 2.6 all_to_all.61
  396.0 6.6 %fusion.20 = f32[1,4,256,256]{3,2,1,0:T(8,128)} fusion(f32[1,4,256,256]{3,2,1,0:T(8,128)S(1)} %copy-done.3, f32[1,4,256,256]{3,2,1,0:T(8,128)} %fusion.22, f32[4,256,256]{2,1,0:T(8,128)S(1)} %copy-done.4, f32[1,4,256,256]{3,2,1,0:T(8,128)S(1)} %copy-done.6, f32[]{:T(128)} %bitcast.28, f32[]{:T(128)} %bitcast.27, f32[]{:T(128)} %bitcast, ...), kind=kOutput, calls=%fused_computation.34 | convolution fusion | flops 811270144 | bytes 7340044 | tf_op jit(solution)/shard_map/dot_general | solution.py:90
  402.5 176.8 %all-gather.2.cloned.1.call-done = f32[8,4,256,256]{3,2,1,0:T(8,128)} async-done(((f32[1,4,256,256]{3,2,1,0:T(8,128)}), f32[8,4,256,256]{3,2,1,0:T(8,128)}) %all-gather.2.cloned.1.call-update) | async-done | bytes 8388624 | tf_op jit(solution)/shard_map/all_gather | solution.py:106
  579.3 4.1 reduce_sum.8
  (72 shorter events, 47.8 us)
Async XLA Ops:
  6.5 156.5 %copy-start = (f32[16,4,128]{2,1,0:T(4,128)S(1)}, f32[16,4,128]{2,1,0:T(4,128)}, u32[]{:S(2)}) copy-start(f32[16,4,128]{2,1,0:T(4,128)} %param.17) | copy-start | bytes 98308
  82.3 11.6 %copy-start.1 = (f32[1,4,256,256]{3,2,1,0:T(8,128)S(1)}, f32[1,4,256,256]{3,2,1,0:T(8,128)}, u32[]{:S(2)}) copy-start(f32[1,4,256,256]{3,2,1,0:T(8,128)} %param.14) | copy-start | bytes 3145732
  84.0 16.5 %copy-start.7 = (s32[16,2,128]{2,1,0:T(2,128)S(1)}, s32[16,2,128]{2,1,0:T(2,128)}, u32[]{:S(2)}) copy-start(s32[16,2,128]{2,1,0:T(2,128)} %param.16) | copy-start | bytes 49156
  84.0 113.8 %all-to-all-start.1 = ((f32[1,256,4,256]{3,2,0,1:T(4,128)}), f32[1,256,4,256]{3,2,0,1:T(4,128)}, u32[]{:S(2)}, u32[]{:S(2)}) async-start(f32[1,256,4,256]{3,2,0,1:T(4,128)} %copy.22), calls=%async_computation.1 | async-start | bytes 2097152 | tf_op jit(solution)/shard_map/all_to_all | solution.py:64
  95.0 52.6 %collective-permute-start = (f32[1,3,256,256]{3,2,1,0:T(8,128)}, f32[1,3,256,256]{3,2,1,0:T(8,128)S(1)}, u32[]{:S(2)}, u32[]{:S(2)}) collective-permute-start(f32[1,3,256,256]{3,2,1,0:T(8,128)} %get-tuple-element.59), channel_id=1, source_target_pairs={{0,1},{1,2},{2,3},{3,4},{4,5},{5,6},{6,7},{7,8},{8,9},{9,10},{10,1... | collective-permute-start | bytes 2359304 | tf_op jit(solution)/shard_map/ppermute | solution.py:21
  98.6 51.1 %collective-permute-start.1 = (f32[1,3,256,256]{3,2,1,0:T(8,128)S(1)}, f32[1,3,256,256]{3,2,1,0:T(8,128)S(1)}, u32[]{:S(2)}, u32[]{:S(2)}) collective-permute-start(f32[1,3,256,256]{3,2,1,0:T(8,128)S(1)} %get-tuple-element.60), channel_id=1, source_target_pairs={{1,0},{2,1},{3,2},{4,3},{5,4},{6,5},{7,6},{8,7},{9,8},{10,9},{11,1... | collective-permute-start | bytes 2359304 | tf_op jit(solution)/shard_map/ppermute | solution.py:23
  151.2 12.1 %copy-start.9 = (f32[4]{0:T(128)S(1)}, f32[4]{0:T(128)}, u32[]{:S(2)}) copy-start(f32[4]{0:T(128)} %param.18) | copy-start | bytes 52
  177.5 11.1 %copy-start.2 = (f32[1,4,256,256]{3,2,1,0:T(8,128)S(1)}, f32[1,4,256,256]{3,2,1,0:T(8,128)}, u32[]{:S(2)}) copy-start(f32[1,4,256,256]{3,2,1,0:T(8,128)} %param.14) | copy-start | bytes 3145732
  180.3 11.7 %collective-permute-start.2 = (f32[1,3,256,256]{3,2,1,0:T(8,128)}, f32[1,3,256,256]{3,2,1,0:T(8,128)}, u32[]{:S(2)}, u32[]{:S(2)}) collective-permute-start(f32[1,3,256,256]{3,2,1,0:T(8,128)} %get-tuple-element.56), channel_id=1, source_target_pairs={{63,0},{0,1},{1,2},{2,3},{3,4},{4,5},{5,6},{6,7},{7,8},{8,9},{9,10... | collective-permute-start | bytes 2359304 | tf_op jit(solution)/shard_map/ppermute | solution.py:33
  182.6 13.9 %collective-permute-start.3 = (f32[1,3,256,256]{3,2,1,0:T(8,128)}, f32[1,3,256,256]{3,2,1,0:T(8,128)}, u32[]{:S(2)}, u32[]{:S(2)}) collective-permute-start(f32[1,3,256,256]{3,2,1,0:T(8,128)} %get-tuple-element.55), channel_id=1, source_target_pairs={{1,0},{2,1},{3,2},{4,3},{5,4},{6,5},{7,6},{8,7},{9,8},{10,9},{11,1... | collective-permute-start | bytes 2359304 | tf_op jit(solution)/shard_map/ppermute | solution.py:33
  190.7 1.3 slice-start
  277.3 113.6 %all-to-all-start.3 = ((f32[1,256,4,256]{3,2,0,1:T(4,128)}), f32[1,256,4,256]{3,2,0,1:T(4,128)}, u32[]{:S(2)}, u32[]{:S(2)}) async-start(f32[1,256,4,256]{3,2,0,1:T(4,128)} %copy.27), calls=%async_computation.3 | async-start | bytes 2097152 | tf_op jit(solution)/shard_map/all_to_all | solution.py:64
  287.1 292.2 %all-gather.2.cloned.1.call-start = ((), (), s32[]{:S(2)}) async-start(), calls=%async_computation.4 | async-start | bytes 9437184 | tf_op jit(solution)/shard_map/all_gather | solution.py:106
  287.3 53.3 %collective-permute-start.4 = (f32[1,3,256,256]{3,2,1,0:T(8,128)S(1)}, f32[1,3,256,256]{3,2,1,0:T(8,128)S(1)}, u32[]{:S(2)}, u32[]{:S(2)}) collective-permute-start(f32[1,3,256,256]{3,2,1,0:T(8,128)S(1)} %get-tuple-element.57), channel_id=1, source_target_pairs={{0,1},{1,2},{2,3},{3,4},{4,5},{5,6},{6,7},{7,8},{8,9},{9,10},{10,1... | collective-permute-start | bytes 2359304 | tf_op jit(solution)/shard_map/ppermute | solution.py:21
  290.8 52.0 %collective-permute-start.5 = (f32[1,3,256,256]{3,2,1,0:T(8,128)S(1)}, f32[1,3,256,256]{3,2,1,0:T(8,128)S(1)}, u32[]{:S(2)}, u32[]{:S(2)}) collective-permute-start(f32[1,3,256,256]{3,2,1,0:T(8,128)S(1)} %get-tuple-element.58), channel_id=1, source_target_pairs={{1,0},{2,1},{3,2},{4,3},{5,4},{6,5},{7,6},{8,7},{9,8},{10,9},{11,1... | collective-permute-start | bytes 2359304 | tf_op jit(solution)/shard_map/ppermute | solution.py:23
  372.4 8.4 %copy-start.8 = (f32[3]{0:T(128)S(1)}, f32[3]{0:T(128)}, u32[]{:S(2)}) copy-start(f32[3]{0:T(128)} %param.19) | copy-start | bytes 40
  372.5 9.7 %copy-start.5 = (f32[1,4,256,256]{3,2,1,0:T(8,128)S(1)}, f32[1,4,256,256]{3,2,1,0:T(8,128)}, u32[]{:S(2)}) copy-start(f32[1,4,256,256]{3,2,1,0:T(8,128)} %get-tuple-element.65) | copy-start | bytes 3145732
  372.7 13.7 %collective-permute-start.6 = (f32[1,3,256,256]{3,2,1,0:T(8,128)S(1)}, f32[1,3,256,256]{3,2,1,0:T(8,128)S(1)}, u32[]{:S(2)}, u32[]{:S(2)}) collective-permute-start(f32[1,3,256,256]{3,2,1,0:T(8,128)S(1)} %get-tuple-element.54), channel_id=1, source_target_pairs={{63,0},{0,1},{1,2},{2,3},{3,4},{4,5},{5,6},{6,7},{7,8},{8,9},{9,10... | collective-permute-start | bytes 2359304 | tf_op jit(solution)/shard_map/ppermute | solution.py:33
  375.1 13.6 %collective-permute-start.7 = (f32[1,3,256,256]{3,2,1,0:T(8,128)S(1)}, f32[1,3,256,256]{3,2,1,0:T(8,128)S(1)}, u32[]{:S(2)}, u32[]{:S(2)}) collective-permute-start(f32[1,3,256,256]{3,2,1,0:T(8,128)S(1)} %get-tuple-element.53), channel_id=1, source_target_pairs={{1,0},{2,1},{3,2},{4,3},{5,4},{6,5},{7,6},{8,7},{9,8},{10,9},{11,1... | collective-permute-start | bytes 2359304 | tf_op jit(solution)/shard_map/ppermute | solution.py:33
  390.8 5.1 copy-start.3
  390.8 5.1 copy-start.4
  390.8 5.1 copy-start.6
Sparse Core Ops, SparseCore 0:
  402.7 176.5 all-gather.1
